TPU v7x, 32 devices: a whole 2x2x4 slice. The times are simulated.
32 devices in a mesh: py: 4 (over z), pz: 8 (over y, x, core).
Axes of the slice: x: 2, y: 2, z: 4, core: 2. Of those that a mesh axis runs over, the one named last changes fastest.
Arguments:
- vort_p: bfloat16 [3, 131072], P(None, ('py', 'pz')), may hold values from -6 to 6
- pair_weights: bfloat16 [8192, 64, 128], P(('py', 'pz')), may hold values from -1.796875 to 1.796875
- pair_part: int32 [8192], P(('py', 'pz')), may hold values from 0 to 31
- pair_node: int32 [8192], P(('py', 'pz')), may hold values from 0 to 95, as said below
- counts: int32 [32], P(('py', 'pz')), may hold values from 128 to 256, as said below
Outputs:
- vel_p: float32 [3, 131072], P(None, ('py', 'pz'))
Inputs may be any that keep to these rules, and one draw needn't show every extreme that they name: `counts`: every pencil has at least 128 live slots, and some pencil has all 256 slots live in every draw. `pair_node`: in every pencil the slots below 96 name each of its node blocks exactly once.
All inputs are finite; a program needn't handle non-finite values.
Results may differ from a plain program's by a relative error of at most 0.0029.
Values sent between devices are 32-bit elements; how exact they have to be, the bound alone decides.
A program may use at most 64 MiB of HBM per device.

v0:
```python
import math

import jax
import jax.numpy as jnp
from jax import lax
from jax.sharding import PartitionSpec as P

NX = 384
CY = 8
CZ = 2
BP = 128
BN = 64
PB_DEV = 32


def twiddle(row_index, col_index, period):
    product = row_index[:, None] * col_index[None, :] % period
    return product.astype(jnp.float32) * (2.0 * math.pi / period)


def forward_table(length):
    angle = twiddle(jnp.arange(length), jnp.arange(length), length)
    cosine = jnp.cos(angle)
    sines = jnp.sin(angle)
    return jnp.stack([jnp.stack([cosine, -sines], 1), jnp.stack([sines, cosine], 1)], 0)


def inverse_table(length):
    angle = twiddle(jnp.arange(length), jnp.arange(length), length)
    cosine = jnp.cos(angle) / length
    sines = jnp.sin(angle) / length
    return jnp.stack([jnp.stack([cosine, sines], 1), jnp.stack([-sines, cosine], 1)], 0)


def cross_terms(coeffs, field):
    return jnp.stack(
        [
            coeffs[1] * field[2] - coeffs[2] * field[1],
            coeffs[2] * field[0] - coeffs[0] * field[2],
            coeffs[0] * field[1] - coeffs[1] * field[0],
        ],
        axis=0,
    )


def signed_wave(length, index):
    signed = jnp.where(index < length // 2, index, index - length)
    return (signed.astype(jnp.float32) * (2.0 * math.pi / length), index == length // 2)


def curl_solve(spectrum, y_cells, z_cells):
    x_local = spectrum.shape[1]
    y_local = spectrum.shape[3]
    mode_x = lax.axis_index("py") * x_local + jnp.arange(x_local)
    wave_x = mode_x.astype(jnp.float32) * (2.0 * math.pi / NX)
    wave_y, edge_y = signed_wave(y_cells, lax.axis_index("pz") * y_local + jnp.arange(y_local))
    wave_z, edge_z = signed_wave(z_cells, jnp.arange(z_cells))
    wave_x3 = wave_x[:, None, None]
    wave_y3 = wave_y[None, :, None]
    wave_z3 = wave_z[None, None, :]
    total = wave_x3 * wave_x3 + wave_y3 * wave_y3 + wave_z3 * wave_z3
    edges = edge_y[None, :, None] | edge_z[None, None, :]
    keep = (total > 0) & jnp.logical_not(edges)
    inverse_sq = jnp.where(keep, 1.0 / jnp.where(keep, total, 1.0), 0.0)
    inv_wave = (wave_x3 * inverse_sq, wave_y3 * inverse_sq, wave_z3 * inverse_sq)
    real_turn = cross_terms(inv_wave, spectrum[:, :, 0])
    imag_turn = cross_terms(inv_wave, spectrum[:, :, 1])
    return jnp.stack([-imag_turn, real_turn], axis=2)


def per_device(vort_p, pair_weights, pair_part, pair_node, counts):
    highest = lax.Precision.HIGHEST
    y_cells = CY * lax.axis_size("py")
    z_cells = CZ * lax.axis_size("pz")
    x_modes = NX // 2
    node_blocks = NX * CY * CZ // BN
    pair_slots = pair_weights.shape[0]
    live_mask = (jnp.arange(pair_slots) < counts[0]).astype(jnp.float32)
    particle_blocks = vort_p.reshape(3, PB_DEV, BP).transpose(1, 0, 2)
    picked = particle_blocks[pair_part]
    products = jnp.einsum("pcq,pnq->pcn", picked, pair_weights, preferred_element_type=jnp.float32)
    products = products * live_mask[:, None, None]
    node_sums = jax.ops.segment_sum(products, pair_node, num_segments=node_blocks)
    vort_grid = node_sums.transpose(1, 0, 2).reshape(3, CZ, CY, NX)
    angle_fwd = twiddle(jnp.arange(NX), jnp.arange(x_modes), NX)
    x_forward = jnp.stack([jnp.cos(angle_fwd), -jnp.sin(angle_fwd)], 1)
    angle_inv = twiddle(jnp.arange(x_modes), jnp.arange(NX), NX)
    mode_weight = (jnp.where(jnp.arange(x_modes) == 0, 1.0, 2.0) / NX)[:, None]
    x_inverse = jnp.stack([mode_weight * jnp.cos(angle_inv), -mode_weight * jnp.sin(angle_inv)], 0)
    y_forward = forward_table(y_cells)
    z_forward = forward_table(z_cells)
    z_inverse = inverse_table(z_cells)
    y_inverse = inverse_table(y_cells)
    x_spectrum = jnp.einsum("czyx,xrm->czrmy", vort_grid, x_forward, precision=highest)
    row_section = jnp.einsum(
        "czrmy,rysk->cmskz",
        lax.all_to_all(x_spectrum, "py", split_axis=3, concat_axis=4, tiled=True),
        y_forward,
        precision=highest,
    )
    col_section = jnp.einsum(
        "cmrkz,rzsw->cmskw",
        lax.all_to_all(row_section, "pz", split_axis=3, concat_axis=4, tiled=True),
        z_forward,
        precision=highest,
    )
    vel_spectrum = curl_solve(col_section, y_cells, z_cells)
    z_back = jnp.einsum("cmrkw,rwsz->cmszk", vel_spectrum, z_inverse, precision=highest)
    y_back = jnp.einsum(
        "cmrzk,rksy->czsym",
        lax.all_to_all(z_back, "pz", split_axis=3, concat_axis=4, tiled=True),
        y_inverse,
        precision=highest,
    )
    vel_grid = jnp.einsum(
        "czrym,rmx->czyx",
        lax.all_to_all(y_back, "py", split_axis=3, concat_axis=4, tiled=True),
        x_inverse,
        precision=highest,
    )
    vel_nodes = vel_grid.astype(jnp.bfloat16).reshape(3, node_blocks, BN).transpose(1, 0, 2)
    chosen = vel_nodes[pair_node]
    back_products = jnp.einsum(
        "pcn,pnq->pcq", chosen, pair_weights, preferred_element_type=jnp.float32
    )
    back_products = back_products * live_mask[:, None, None]
    block_sums = jax.ops.segment_sum(back_products, pair_part, num_segments=PB_DEV)
    return block_sums.transpose(1, 0, 2).reshape(3, PB_DEV * BP)


def solution(mesh):
    placed = (
        P(None, ("py", "pz")),
        P(("py", "pz"), None, None),
        P(("py", "pz")),
        P(("py", "pz")),
        P(("py", "pz")),
    )
    return jax.shard_map(
        per_device, mesh=mesh, in_specs=placed, out_specs=P(None, ("py", "pz")), check_vma=False
    )
```

profile of v0, /device:TPU:0, one launch (start us, length us, event | category | flops | bytes accessed | tf_op | source)
XLA Modules:
  0.0 85.7 jit_solution(18046302165905745508)
XLA Ops:
  0.0 0.0 copy-start
  0.0 1.2 %sine_negate_fusion = (f32[384,1,192]{0,2,1:T(8,128)S(1)}, f32[384,1,192]{0,2,1:T(8,128)S(1)}) fusion(), kind=kLoop, calls=%fused_computation.30 | loop fusion | flops 737280 | bytes 589824 | tf_op jit(solution)/shard_map/neg | solution.py:86
  1.9 0.7 compare_select_fusion.1
  2.6 1.0 %gather_fusion = bf16[256,3,128]{2,1,0:T(4,128)(2,1)S(1)} fusion(bf16[32,3,128]{2,1,0:T(4,128)(2,1)S(1)} %bitcast.162, s32[1024]{0:T(1024)S(1)} %pad_clamp_fusion.1), kind=kCustom, calls=%fused_computation | custom fusion | bytes 394240 | tf_op jit(solution)/shard_map/gather | solution.py:80
  3.6 4.4 %convolution_multiply_fusion.1 = f32[256,3,64]{2,1,0:T(4,128)S(1)} fusion(bf16[256,3,128]{2,1,0:T(4,128)(2,1)S(1)} %gather_fusion, bf16[256,64,128]{2,1,0:T(8,128)(2,1)} %param.6, f32[256]{0:T(256)S(1)} %compare_convert_fusion), kind=kOutput, calls=%fused_computation.5 | convolution fusion | flops 12632064 | bytes 4588544 | tf_op jit(solution)/shard_map/pcq,pnq->pcn/dot_general | solution.py:81
  8.1 0.0 copy-done.2
  8.1 8.4 %scatter_fusion = f32[96,3,64]{2,1,0:T(4,128)S(1)} fusion(f32[96,3,64]{2,1,0:T(4,128)S(1)} %broadcast_in_dim.24, s32[256]{0:T(256)S(1)} %copy-done.2, f32[256,3,64]{2,1,0:T(4,128)S(1)} %convolution_multiply_fusion.1), kind=kCustom, calls=%fused_computation.2 | custom fusion | flops 49152 | bytes 590848 | tf_op jit(solution)/shard_map/scatter-add | solution.py:83
  16.5 0.1 reshape.719
  16.6 0.9 %convolution_bitcast_fusion.4 = f32[3,2,2,192,8]{3,4,1,0,2:T(8,128)S(1)} fusion(f32[3,2,8,384,1]{3,2,1,0,4:T(8,128)S(1)} %reshape.719, f32[384,1,192]{0,2,1:T(8,128)S(1)} %get-tuple-element.19, f32[384,1,192]{0,2,1:T(8,128)S(1)} %get-tuple-element.20), kind=kOutput, calls=%fused_computation.10 | convolution fusion | flops 85082112 | bytes 737280 | tf_op jit(solution)/shard_map/czyx,xrm->czrmy/dot_general | solution.py:94
  17.4 0.8 copy.33
  18.2 2.5 %reshape.735 = f32[4,1,4608]{2,1,0:T(1,128)} reshape(f32[192,2,3,2,8]{4,3,2,1,0:T(2,128)S(1)} %bitcast.163) | data formatting | bytes 147456
  20.7 6.3 %all-to-all-start = ((f32[4,1,4608]{2,1,0:T(1,128)}), f32[4,1,4608]{2,1,0:T(1,128)S(1)}, u32[]{:S(2)}, u32[]{:S(2)}) async-start(f32[4,1,4608]{2,1,0:T(1,128)} %reshape.735), calls=%async_computation | async-start | bytes 147456 | tf_op jit(solution)/shard_map/all_to_all | solution.py:97
  27.0 0.1 fusion.42
  27.1 0.1 fusion.44
  27.2 0.1 fusion.47
  27.2 0.1 fusion.49
  27.4 0.1 broadcast_multiply_fusion.2
  27.4 0.1 fusion.50
  27.5 0.1 broadcast_multiply_fusion
  27.6 0.1 broadcast_add_fusion
  27.7 0.1 or_not_fusion
  27.8 1.2 %sine_multiply_fusion = (f32[1,192,384]{2,1,0:T(8,128)S(1)}, f32[1,192,384]{2,1,0:T(8,128)S(1)}) fusion(f32[192]{0:T(256)S(1)} %fusion.57, f32[192]{0:T(256)S(1)} %fusion.51), kind=kLoop, calls=%fused_computation.25 | loop fusion | flops 811008 | bytes 591360 | tf_op jit(solution)/shard_map/mul | solution.py:89
  29.1 0.1 fusion.46
  29.1 3.6 %all-to-all-done = f32[4,1,4608]{2,1,0:T(1,128)S(1)} async-done(((f32[4,1,4608]{2,1,0:T(1,128)}), f32[4,1,4608]{2,1,0:T(1,128)S(1)}, u32[]{:S(2)}, u32[]{:S(2)}) %all-to-all-start) | async-done | bytes 73760 | tf_op jit(solution)/shard_map/all_to_all | solution.py:97
  32.8 0.5 broadcast.1152
  33.3 0.8 reduce
  34.1 1.8 %reshape.736 = f32[192,2,3,2,8]{4,3,2,1,0:T(2,128)S(1)} reshape(f32[4,4608]{1,0:T(4,128)S(1)} %reduce) | data formatting | bytes 147456
  35.9 0.7 copy.34
  36.6 0.4 convolution_bitcast_fusion.3
  37.0 0.2 copy.81
  37.2 1.0 %reshape.737 = f32[8,1,2304]{2,1,0:T(1,128)} reshape(f32[32,2,3,2,48]{4,3,2,1,0:T(2,128)S(1)} %bitcast.168) | data formatting | bytes 147456
  38.1 3.7 %all-to-all-start.1 = ((f32[8,1,2304]{2,1,0:T(1,128)}), f32[8,1,2304]{2,1,0:T(1,128)S(1)}, u32[]{:S(2)}, u32[]{:S(2)}) async-start(f32[8,1,2304]{2,1,0:T(1,128)} %reshape.737), calls=%async_computation.1 | async-start | bytes 147456 | tf_op jit(solution)/shard_map/all_to_all | solution.py:103
  41.8 5.1 %all-to-all-done.1 = f32[8,1,2304]{2,1,0:T(1,128)S(1)} async-done(((f32[8,1,2304]{2,1,0:T(1,128)}), f32[8,1,2304]{2,1,0:T(1,128)S(1)}, u32[]{:S(2)}, u32[]{:S(2)}) %all-to-all-start.1) | async-done | bytes 73760 | tf_op jit(solution)/shard_map/all_to_all | solution.py:103
  46.9 0.8 reduce.1
  47.7 0.3 reshape.738
  48.1 0.1 copy.36
  48.2 0.4 convolution_bitcast_fusion.2
  48.5 0.1 multiply_subtract_fusion.5
  48.6 0.1 multiply_subtract_fusion.2
  48.8 0.4 convolution_bitcast_fusion.1
  49.2 0.1 copy.80
  49.3 0.9 %reshape.739 = f32[8,1,2304]{2,1,0:T(1,128)} reshape(f32[16,2,3,4,48]{4,3,2,1,0:T(4,128)S(1)} %bitcast.170) | data formatting | bytes 147456
  50.1 3.5 %all-to-all-start.2 = ((f32[8,1,2304]{2,1,0:T(1,128)}), f32[8,1,2304]{2,1,0:T(1,128)S(1)}, u32[]{:S(2)}, u32[]{:S(2)}) async-start(f32[8,1,2304]{2,1,0:T(1,128)} %reshape.739), calls=%async_computation.2 | async-start | bytes 147456 | tf_op jit(solution)/shard_map/all_to_all | solution.py:111
  53.7 4.8 %all-to-all-done.2 = f32[8,1,2304]{2,1,0:T(1,128)S(1)} async-done(((f32[8,1,2304]{2,1,0:T(1,128)}), f32[8,1,2304]{2,1,0:T(1,128)S(1)}, u32[]{:S(2)}, u32[]{:S(2)}) %all-to-all-start.2) | async-done | bytes 73760 | tf_op jit(solution)/shard_map/all_to_all | solution.py:111
  58.5 0.8 reduce.2
  59.3 0.2 reshape.740
  59.5 0.4 convolution_bitcast_fusion
  59.9 0.0 copy-start.3
  59.9 0.2 copy.79
  60.1 1.0 %reshape.741 = f32[4,1,4608]{2,1,0:T(1,128)} reshape(f32[32,2,3,2,48]{4,3,2,1,0:T(2,128)S(1)} %bitcast.172) | data formatting | bytes 147456
  61.0 3.3 %all-to-all-start.3 = ((f32[4,1,4608]{2,1,0:T(1,128)}), f32[4,1,4608]{2,1,0:T(1,128)S(1)}, u32[]{:S(2)}, u32[]{:S(2)}) async-start(f32[4,1,4608]{2,1,0:T(1,128)} %reshape.741), calls=%async_computation.3 | async-start | bytes 147456 | tf_op jit(solution)/shard_map/all_to_all | solution.py:117
  64.4 5.7 %all-to-all-done.3 = f32[4,1,4608]{2,1,0:T(1,128)S(1)} async-done(((f32[4,1,4608]{2,1,0:T(1,128)}), f32[4,1,4608]{2,1,0:T(1,128)S(1)}, u32[]{:S(2)}, u32[]{:S(2)}) %all-to-all-start.3) | async-done | bytes 73760 | tf_op jit(solution)/shard_map/all_to_all | solution.py:117
  70.1 0.8 reduce.3
  70.9 0.3 reshape.742
  71.3 0.1 copy.77
  71.4 0.1 all_to_all.67
  71.5 0.5 fusion
  72.0 0.1 reshape.680
  72.1 0.1 copy.78
  72.2 1.0 %gather_fusion.1 = bf16[256,3,64]{2,1,0:T(4,128)(2,1)S(1)} fusion(bf16[96,3,64]{2,1,0:T(4,128)(2,1)S(1)} %bitcast.166, s32[1024]{0:T(1024)S(1)} %pad_clamp_fusion), kind=kCustom, calls=%fused_computation.1 | custom fusion | bytes 197632 | tf_op jit(solution)/shard_map/gather | solution.py:122
  73.2 3.4 %convolution_multiply_fusion = f32[256,3,128]{2,1,0:T(4,128)S(1)} fusion(bf16[256,3,64]{2,1,0:T(4,128)(2,1)S(1)} %gather_fusion.1, bf16[256,64,128]{2,1,0:T(8,128)(2,1)} %param.6, f32[256]{0:T(256)S(1)} %compare_convert_fusion), kind=kOutput, calls=%fused_computation.4 | convolution fusion | flops 12681216 | bytes 4686848 | tf_op jit(solution)/shard_map/pcn,pnq->pcq/dot_general | solution.py:123
  76.6 8.5 %scatter_fusion.1 = f32[32,3,128]{2,1,0:T(4,128)S(1)} fusion(f32[32,3,128]{2,1,0:T(4,128)S(1)} %broadcast_in_dim.22, s32[256]{0:T(256)S(1)} %copy-done.3, f32[256,3,128]{2,1,0:T(4,128)S(1)} %convolution_multiply_fusion), kind=kCustom, calls=%fused_computation.3 | custom fusion | flops 98304 | bytes 1180672 | tf_op jit(solution)/shard_map/scatter-add | solution.py:127
  85.1 0.0 copy-start.1
  85.1 0.6 copy-done.1
  (24 shorter events, 0.2 us)
Async XLA Ops:
  0.0 2.6 %copy-start = (bf16[3,4096]{1,0:T(4,128)(2,1)S(1)}, bf16[3,4096]{1,0:T(4,128)(2,1)}, u32[]{:S(2)}) copy-start(bf16[3,4096]{1,0:T(4,128)(2,1)} %param.5) | copy-start | bytes 73732
  0.0 8.1 %copy-start.2 = (s32[256]{0:T(256)S(1)}, s32[256]{0:T(256)}, u32[]{:S(2)}) copy-start(s32[256]{0:T(256)} %param.8) | copy-start | bytes 3076
  20.7 12.1 %all-to-all-start = ((f32[4,1,4608]{2,1,0:T(1,128)}), f32[4,1,4608]{2,1,0:T(1,128)S(1)}, u32[]{:S(2)}, u32[]{:S(2)}) async-start(f32[4,1,4608]{2,1,0:T(1,128)} %reshape.735), calls=%async_computation | async-start | bytes 147456 | tf_op jit(solution)/shard_map/all_to_all | solution.py:97
  38.1 8.8 %all-to-all-start.1 = ((f32[8,1,2304]{2,1,0:T(1,128)}), f32[8,1,2304]{2,1,0:T(1,128)S(1)}, u32[]{:S(2)}, u32[]{:S(2)}) async-start(f32[8,1,2304]{2,1,0:T(1,128)} %reshape.737), calls=%async_computation.1 | async-start | bytes 147456 | tf_op jit(solution)/shard_map/all_to_all | solution.py:103
  50.1 8.4 %all-to-all-start.2 = ((f32[8,1,2304]{2,1,0:T(1,128)}), f32[8,1,2304]{2,1,0:T(1,128)S(1)}, u32[]{:S(2)}, u32[]{:S(2)}) async-start(f32[8,1,2304]{2,1,0:T(1,128)} %reshape.739), calls=%async_computation.2 | async-start | bytes 147456 | tf_op jit(solution)/shard_map/all_to_all | solution.py:111
  59.9 16.7 %copy-start.3 = (s32[256]{0:T(256)S(1)}, s32[256]{0:T(256)}, u32[]{:S(2)}) copy-start(s32[256]{0:T(256)} %param.7) | copy-start | bytes 3076
  61.0 9.0 %all-to-all-start.3 = ((f32[4,1,4608]{2,1,0:T(1,128)}), f32[4,1,4608]{2,1,0:T(1,128)S(1)}, u32[]{:S(2)}, u32[]{:S(2)}) async-start(f32[4,1,4608]{2,1,0:T(1,128)} %reshape.741), calls=%async_computation.3 | async-start | bytes 147456 | tf_op jit(solution)/shard_map/all_to_all | solution.py:117
  85.1 0.6 copy-start.1
where the time goes:
time: 86.3 us; the launch traced here: 85.7 us
  other arithmetic  24.3 us (28%)
  waiting for transfers between devices  19.2 us (22%)
  starting transfers between devices  16.9 us (20%)
  local copies, waits for them, and re-layouts  13.6 us (16%)
  matrix products  10.6 us (12%)
  between operations  1.09 us (1%)
    unnamed x16, local copies, waits for them, and re-layouts  8.58 us
    scatter-add x1, other arithmetic, per_device(): jax.ops.segment_sum(back_products, pair_part, num_segments=PB_DEV)  8.47 us
    scatter-add x1, other arithmetic, per_device(): jax.ops.segment_sum(products, pair_node, num_segments=node_blocks)  8.36 us
    all_to_all x1, starting transfers between devices, per_device(): lax.all_to_all(x_spectrum, 'py', split_axis=3, concat_axis=4, tiled=True)  6.31 us
    all_to_all x1, waiting for transfers between devices, per_device(): lax.all_to_all(y_back, 'py', split_axis=3, concat_axis=4, tiled=True)  5.72 us
    all_to_all x1, waiting for transfers between devices, per_device(): lax.all_to_all(row_section, 'pz', split_axis=3, concat_axis=4, tiled=True)  5.05 us
    all_to_all x1, waiting for transfers between devices, per_device(): lax.all_to_all(z_back, 'pz', split_axis=3, concat_axis=4, tiled=True)  4.8 us
    dot_general x1, matrix products, per_device(): jnp.einsum('pcq,pnq->pcn', picked, pair_weights, preferred_element_type=j...  4.45 us
  transfers between devices with their start and end apart: 4, of which 4 were waited for; matrix products, arithmetic and copies ran while one was open for 2% of the time, Pallas kernels for 0%

commit v1 on v0

--- a/solution.py
+++ b/solution.py
@@ -1,8 +1,12 @@
+import functools
 import math
 
 import jax
 import jax.numpy as jnp
+import numpy as np
 from jax import lax
+from jax.experimental import pallas as pl
+from jax.experimental.pallas import tpu as pltpu
 from jax.sharding import PartitionSpec as P
 
 NX = 384
@@ -11,6 +15,12 @@
 BP = 128
 BN = 64
 PB_DEV = 32
+ROWS = 8
+CHUNK = 32
+GROUP = 16
+MESH = pl.DeviceIdType.MESH
+f32 = jnp.float32
+bf16 = jnp.bfloat16
 
 
 def twiddle(row_index, col_index, period):
@@ -68,20 +78,339 @@
     return jnp.stack([-imag_turn, real_turn], axis=2)
 
 
-def per_device(vort_p, pair_weights, pair_part, pair_node, counts):
+def halves(table):
+    table = np.asarray(table, np.float32)
+    high = table.astype(bf16)
+    return high, (table - high.astype(np.float32)).astype(bf16)
+
+
+def split(x):
+    high = x.astype(bf16)
+    return high, (x - high.astype(f32)).astype(bf16)
+
+
+def dot(a, b, dims=((1,), (0,))):
+    return lax.dot_general(a, b, (dims, ((), ())), preferred_element_type=f32)
+
+
+def spread_kernel(part, node, count, parts_ref, w_ref, out_ref):
+    step = pl.program_id(0)
+
+    @pl.when(step == 0)
+    def _():
+        out_ref[...] = jnp.zeros_like(out_ref)
+
+    def group(g, carry):
+        sums = []
+        for i in range(GROUP):
+            p = g * GROUP + i
+            slot = step * CHUNK + p
+            start = pl.multiple_of(part[slot] * BP, BP)
+            picked = parts_ref[:, pl.ds(start, BP)]
+            got = dot(picked, w_ref[p], ((1,), (1,)))
+            sums.append(jnp.where(slot < count[0], got, 0.0))
+        for i in range(GROUP):
+            j = node[step * CHUNK + g * GROUP + i]
+            out_ref[j, 0:3, :] += sums[i]
+        return carry
+
+    lax.fori_loop(0, CHUNK // GROUP, group, 0)
+
+
+def spread(vort_p, weights, part, node, counts, node_blocks):
+    slots = weights.shape[0]
+    return pl.pallas_call(
+        spread_kernel,
+        out_shape=jax.ShapeDtypeStruct((node_blocks, ROWS, BN), f32),
+        grid_spec=pltpu.PrefetchScalarGridSpec(
+            num_scalar_prefetch=3,
+            grid=(slots // CHUNK,),
+            in_specs=[
+                pl.BlockSpec(vort_p.shape, lambda i, *_: (0, 0)),
+                pl.BlockSpec((CHUNK, BN, BP), lambda i, *_: (i, 0, 0)),
+            ],
+            out_specs=pl.BlockSpec((node_blocks, ROWS, BN), lambda i, *_: (0, 0, 0)),
+        ),
+        name="spread",
+    )(part, node, counts, vort_p, weights)
+
+
+def collect_kernel(part, node, count, vel_ref, w_ref, out_ref, sums_ref):
+    step = pl.program_id(0)
+
+    @pl.when(step == 0)
+    def _():
+        sums_ref[...] = jnp.zeros_like(sums_ref)
+
+    def group(g, carry):
+        sums = []
+        for i in range(GROUP):
+            p = g * GROUP + i
+            slot = step * CHUNK + p
+            chosen = vel_ref[node[slot]].astype(bf16)
+            got = dot(chosen, w_ref[p])
+            sums.append(jnp.where(slot < count[0], got, 0.0))
+        for i in range(GROUP):
+            b = part[step * CHUNK + g * GROUP + i]
+            sums_ref[b] += sums[i]
+        return carry
+
+    lax.fori_loop(0, CHUNK // GROUP, group, 0)
+
+    @pl.when(step == pl.num_programs(0) - 1)
+    def _():
+        for b in range(PB_DEV):
+            out_ref[:, b * BP : (b + 1) * BP] = sums_ref[b, 0:3, :]
+
+
+def collect(vel, weights, part, node, counts):
+    slots = weights.shape[0]
+    return pl.pallas_call(
+        collect_kernel,
+        out_shape=jax.ShapeDtypeStruct((3, PB_DEV * BP), f32),
+        grid_spec=pltpu.PrefetchScalarGridSpec(
+            num_scalar_prefetch=3,
+            grid=(slots // CHUNK,),
+            in_specs=[
+                pl.BlockSpec(vel.shape, lambda i, *_: (0, 0, 0)),
+                pl.BlockSpec((CHUNK, BN, BP), lambda i, *_: (i, 0, 0)),
+            ],
+            out_specs=pl.BlockSpec((3, PB_DEV * BP), lambda i, *_: (0, 0)),
+            scratch_shapes=[pltpu.VMEM((PB_DEV, ROWS, BP), f32)],
+        ),
+        name="collect",
+    )(part, node, counts, vel, weights)
+
+
+def tables(n_py, n_pz):
+    devices = n_py * n_pz
+    local = NX // 2 // devices
+    ny, nz = CY * n_py, CZ * n_pz
+    row = np.arange(devices * ROWS)
+    slot, device = row % ROWS, row // ROWS
+    mode = device * local + slot
+    angle = 2 * np.pi * (mode[:, None] * np.arange(NX)[None] % NX) / NX
+    used = (slot < local)[:, None]
+    x_cos, x_sin = np.where(used, np.cos(angle), 0.0), np.where(used, -np.sin(angle), 0.0)
+    index = np.arange(devices)
+    a, b = index // n_pz, index % n_pz
+    theta = 2 * np.pi * (a[:, None] * a[None] / n_py + b[:, None] * b[None] / n_pz)
+    eye = np.eye(ROWS)
+    far = np.concatenate([np.kron(np.cos(theta), eye), np.kron(np.sin(theta), eye)], 0)
+    lane = np.arange(128)
+    real, comp, cell = lane // 64, lane % 64 // 16, lane % 16
+    zl, yl = cell // CY, cell % CY
+    valid = (comp < 3)[None]
+    phi = 2 * np.pi * (a[:, None] * yl[None] / ny + b[:, None] * zl[None] / nz)
+    sign = np.where(real == 0, 1.0, -1.0)[None]
+    turn_cos, turn_sin = np.cos(phi), np.sin(phi) * sign
+    psi = 2 * np.pi * (yl[:, None] * yl[None] / CY + zl[:, None] * zl[None] / CZ)
+
+    def near(ahead):
+        cosine, sines = np.cos(psi), np.sin(psi)
+        r, q = real[:, None], real[None]
+        both = np.where(r == q, sines, np.where(r == 0, cosine, -cosine))
+        same = (comp[:, None] == (comp[None] + ahead) % 3) & (comp[:, None] < 3) & valid
+        return np.where(same, both, 0.0)
+
+    forward = np.concatenate([near(2), near(1)], 1)
+    cosine, sines = np.cos(psi), np.sin(psi)
+    r, q = real[:, None], real[None]
+    both = np.where(r == q, cosine, np.where(r == 0, sines, -sines))
+    same = (comp[:, None] == comp[None]) & (comp[:, None] < 3)
+    back = np.where(same, both, 0.0)
+    my, mz = a[:, None] + n_py * yl[None], b[:, None] + n_pz * zl[None]
+    keep = (my != ny // 2) & (mz != nz // 2) & valid
+    my, mz = np.where(my < ny // 2, my, my - ny), np.where(mz < nz // 2, mz, mz - nz)
+    ky, kz = 2 * np.pi * my / ny, 2 * np.pi * mz / nz
+    zero = np.zeros_like(ky)
+    wave = np.stack([zero, ky, kz])
+    k_first = np.where(comp == 0, wave[1], np.where(comp == 1, wave[2], wave[0]))
+    k_second = np.where(comp == 0, wave[2], np.where(comp == 1, wave[0], wave[1]))
+    x_first = np.broadcast_to(comp == 2, ky.shape)
+    x_second = np.broadcast_to(comp == 1, ky.shape)
+    small = [turn_cos, turn_sin, ky * ky + kz * kz, k_first, k_second, x_first, x_second, keep]
+    small = np.stack(small).astype(np.float32)
+    return [
+        *halves(np.stack([x_cos, x_sin])),
+        *halves(far),
+        *halves(forward),
+        *halves(back),
+        small,
+    ]
+
+
+def solve_kernel(
+    n_py,
+    n_pz,
+    grid_ref,
+    xh_ref,
+    xl_ref,
+    far_h,
+    far_l,
+    fwd_h,
+    fwd_l,
+    back_h,
+    back_l,
+    small,
+    out_ref,
+    send_a,
+    recv_a,
+    send_b,
+    recv_b,
+    send_sem,
+    recv_sem,
+):
+    devices = n_py * n_pz
+    local = NX // 2 // devices
+    rows = devices * ROWS
+    per_row = NX // BN
+    cells = CY * CZ
+    me = lax.axis_index("py") * n_pz + lax.axis_index("pz")
+    barrier = pltpu.get_barrier_semaphore()
+
+    def greet(k, carry):
+        other = lax.rem(me + k, devices)
+        pl.semaphore_signal(
+            barrier, inc=1, device_id=(other // n_pz, lax.rem(other, n_pz)), device_id_type=MESH
+        )
+        return carry
+
+    lax.fori_loop(1, devices, greet, 0)
+
+    def exchange(send, recv, phase):
+        def copy(k, carry):
+            other = lax.rem(me + k, devices)
+            pltpu.make_async_remote_copy(
+                src_ref=send.at[other],
+                dst_ref=recv.at[me],
+                send_sem=send_sem.at[phase],
+                recv_sem=recv_sem.at[phase],
+                device_id=(other // n_pz, lax.rem(other, n_pz)),
+                device_id_type=MESH,
+            ).start()
+            return carry
+
+        lax.fori_loop(1, devices, copy, 0)
+
+    def finish(send, recv, phase):
+        many = pl.ds(0, devices - 1)
+        pltpu.make_async_copy(recv.at[many], recv.at[many], recv_sem.at[phase]).wait()
+
+    def drain(send, phase):
+        many = pl.ds(0, devices - 1)
+        pltpu.make_async_copy(send.at[many], send.at[many], send_sem.at[phase]).wait()
+
+    lines = []
+    for c in range(3):
+        pieces = [
+            grid_ref[pl.ds(xb * ROWS + c, cells, stride=per_row * ROWS), :]
+            for xb in range(per_row)
+        ]
+        lines.append(jnp.concatenate(pieces, axis=1))
+    vort = jnp.concatenate(lines, axis=0)
+    low = jnp.concatenate([vort, jnp.zeros((80, NX), f32)], axis=0)
+    up = jnp.concatenate([jnp.zeros((64, NX), f32), vort, jnp.zeros((16, NX), f32)], axis=0)
+    over = ((1,), (1,))
+    modes = jnp.zeros((rows, 128), f32)
+    for k, field in ((0, low), (1, up)):
+        high, rest = split(field)
+        modes += dot(xh_ref[k], high, over) + (
+            dot(xh_ref[k], rest, over) + dot(xl_ref[k], high, over)
+        )
+    send_a[...] = modes.reshape(devices, ROWS, 128)
+    recv_a[me] = send_a[me]
+    pl.semaphore_wait(barrier, devices - 1)
+    exchange(send_a, recv_a, 0)
+
+    def spread_out(i):
+        return jnp.broadcast_to(small[i][:, None, :], (devices, ROWS, 128)).reshape(rows, 128)
+
+    slot = lax.broadcasted_iota(jnp.int32, (rows, 128), 0) % ROWS
+    mode = me * local + slot
+    wave_x = mode.astype(f32) * (2.0 * math.pi / NX)
+    total = spread_out(2) + wave_x * wave_x
+    ny_nz = CY * n_py * CZ * n_pz
+    weight = jnp.where(mode == 0, 1.0, 2.0) * (1.0 / (NX * ny_nz))
+    inverse = spread_out(7) * weight / jnp.where(total > 0, total, 1.0)
+    gain_a = (spread_out(3) + wave_x * spread_out(5)) * inverse
+    gain_b = (spread_out(4) + wave_x * spread_out(6)) * inverse
+    turn_cos, turn_sin = spread_out(0), spread_out(1)
+    sign = jnp.where(lax.broadcasted_iota(jnp.int32, (rows, 128), 1) < 64, 1.0, -1.0)
+
+    def swap(x):
+        return pltpu.roll(x, 64, 1)
+
+    def across(x):
+        high, rest = split(x)
+        both = dot(far_h[...], high) + (dot(far_h[...], rest) + dot(far_l[...], high))
+        return both[:rows], swap(both[rows:]) * sign
+
+    def along(x, table_h, table_l):
+        high, rest = split(x)
+        return dot(high, table_h[...]) + (dot(rest, table_h[...]) + dot(high, table_l[...]))
+
+    finish(send_a, recv_a, 0)
+    even, odd = across(recv_a[...].reshape(rows, 128))
+    y = even + odd
+    z = turn_cos * y + turn_sin * swap(y)
+    both = along(z, fwd_h, fwd_l)
+    vel = gain_a * both[:, :128] - gain_b * both[:, 128:]
+    y = along(vel, back_h, back_l)
+    z = turn_cos * y - turn_sin * swap(y)
+    even, odd = across(z)
+    send_b[...] = (even - odd).reshape(devices, ROWS, 128)
+    recv_b[me] = send_b[me]
+    exchange(send_b, recv_b, 1)
+    drain(send_a, 0)
+    finish(send_b, recv_b, 1)
+    back = recv_b[...].reshape(rows, 128).T
+    grid = jnp.zeros((48, NX), f32)
+    for k in range(2):
+        high, rest = split(back[64 * k : 64 * k + 48])
+        grid += dot(high, xh_ref[k]) + (dot(rest, xh_ref[k]) + dot(high, xl_ref[k]))
+    grid = grid.astype(bf16).astype(f32)
+    for c in range(3):
+        for xb in range(per_row):
+            out_ref[pl.ds(xb * ROWS + c, cells, stride=per_row * ROWS), :] = grid[
+                c * cells : (c + 1) * cells, xb * BN : (xb + 1) * BN
+            ]
+    drain(send_b, 1)
+
+
+def solve_direct(sums, n_py, n_pz):
+    devices = n_py * n_pz
+    vmem = pl.BlockSpec(memory_space=pltpu.VMEM)
+    block = pltpu.VMEM((devices, ROWS, 128), f32)
+    consts = tables(n_py, n_pz)
+    flat = sums.reshape(-1, BN)
+    out = pl.pallas_call(
+        functools.partial(solve_kernel, n_py, n_pz),
+        out_shape=jax.ShapeDtypeStruct(flat.shape, f32),
+        in_specs=[vmem] * (1 + len(consts)),
+        out_specs=vmem,
+        scratch_shapes=[
+            block,
+            block,
+            block,
+            block,
+            pltpu.SemaphoreType.DMA((2,)),
+            pltpu.SemaphoreType.DMA((2,)),
+        ],
+        compiler_params=pltpu.CompilerParams(
+            collective_id=0, has_side_effects=True, vmem_limit_bytes=32 * 2**20
+        ),
+        name="solve",
+    )(flat, *[jnp.asarray(t) for t in consts])
+    return out.reshape(sums.shape)
+
+
+def solve_staged(sums, n_py, n_pz):
     highest = lax.Precision.HIGHEST
-    y_cells = CY * lax.axis_size("py")
-    z_cells = CZ * lax.axis_size("pz")
+    node_blocks = sums.shape[0]
+    y_cells, z_cells = CY * n_py, CZ * n_pz
     x_modes = NX // 2
-    node_blocks = NX * CY * CZ // BN
-    pair_slots = pair_weights.shape[0]
-    live_mask = (jnp.arange(pair_slots) < counts[0]).astype(jnp.float32)
-    particle_blocks = vort_p.reshape(3, PB_DEV, BP).transpose(1, 0, 2)
-    picked = particle_blocks[pair_part]
-    products = jnp.einsum("pcq,pnq->pcn", picked, pair_weights, preferred_element_type=jnp.float32)
-    products = products * live_mask[:, None, None]
-    node_sums = jax.ops.segment_sum(products, pair_node, num_segments=node_blocks)
-    vort_grid = node_sums.transpose(1, 0, 2).reshape(3, CZ, CY, NX)
+    vort_grid = sums[:, :3].transpose(1, 0, 2).reshape(3, CZ, CY, NX)
     angle_fwd = twiddle(jnp.arange(NX), jnp.arange(x_modes), NX)
     x_forward = jnp.stack([jnp.cos(angle_fwd), -jnp.sin(angle_fwd)], 1)
     angle_inv = twiddle(jnp.arange(x_modes), jnp.arange(NX), NX)
@@ -118,14 +447,19 @@
         x_inverse,
         precision=highest,
     )
-    vel_nodes = vel_grid.astype(jnp.bfloat16).reshape(3, node_blocks, BN).transpose(1, 0, 2)
-    chosen = vel_nodes[pair_node]
-    back_products = jnp.einsum(
-        "pcn,pnq->pcq", chosen, pair_weights, preferred_element_type=jnp.float32
-    )
-    back_products = back_products * live_mask[:, None, None]
-    block_sums = jax.ops.segment_sum(back_products, pair_part, num_segments=PB_DEV)
-    return block_sums.transpose(1, 0, 2).reshape(3, PB_DEV * BP)
+    vel_nodes = vel_grid.astype(bf16).astype(f32).reshape(3, node_blocks, BN).transpose(1, 0, 2)
+    return jnp.pad(vel_nodes, ((0, 0), (0, ROWS - 3), (0, 0)))
+
+
+def per_device(vort_p, pair_weights, pair_part, pair_node, counts):
+    n_py, n_pz = lax.axis_size("py"), lax.axis_size("pz")
+    node_blocks = NX * CY * CZ // BN
+    sums = spread(vort_p, pair_weights, pair_part, pair_node, counts, node_blocks)
+    x_modes = NX // 2
+    devices = n_py * n_pz
+    direct = devices <= 32 and x_modes % devices == 0 and x_modes // devices <= ROWS
+    vel = (solve_direct if direct else solve_staged)(sums, n_py, n_pz)
+    return collect(vel, pair_weights, pair_part, pair_node, counts)
 
 
 def solution(mesh):

time: 86.3 us -> 39 us (0.45)
  Pallas kernels: 0 us -> 36 us
  other arithmetic: 24.3 us -> 0 us
  waiting for transfers between devices: 19.2 us -> 0 us
  starting transfers between devices: 16.9 us -> 0 us
  local copies, waits for them, and re-layouts: 13.6 us -> 1.78 us
  matrix products: 10.6 us -> 0 us
    pallas_call x0 -> x3, Pallas kernels: none -> 36 us  [the longest x1 19.8 us: solve_direct(): pl.pallas_call(functools.partial(solve_kernel, n_py, n_pz), out_shape=jax...]
    all_to_all x4 -> x0, waiting for transfers between devices: 19.2 us -> none  [the longest x1 5.72 us: per_device(): lax.all_to_all(y_back, 'py', split_axis=3, concat_axis=4, tiled=True)]
    all_to_all x4 -> x0, starting transfers between devices: 16.9 us -> none  [the longest x1 6.31 us: per_device(): lax.all_to_all(x_spectrum, 'py', split_axis=3, concat_axis=4, tiled=True)]
    scatter-add x2 -> x0, other arithmetic: 16.8 us -> none  [the longest x1 8.47 us: per_device(): jax.ops.segment_sum(back_products, pair_part, num_segments=PB_DEV)]
    dot_general x8 -> x0, matrix products: 10.6 us -> none  [the longest x1 4.45 us: per_device(): jnp.einsum('pcq,pnq->pcn', picked, pair_weights, preferred_element_type=j...]
    unnamed x16 -> x22, local copies, waits for them, and re-layouts: 8.58 us -> 1.78 us
    all_to_all x4 -> x0, other arithmetic: 3.3 us -> none  [the longest x1 0.83 us: per_device(): lax.all_to_all(y_back, 'py', split_axis=3, concat_axis=4, tiled=True)]
    gather x2 -> x0, local copies, waits for them, and re-layouts: 1.96 us -> none  [the longest x1 0.98 us: per_device(): chosen = vel_nodes[pair_node]]
  transfers between devices with their start and end apart: 4 -> 0, of which waited for: 4 -> 0; matrix products, arithmetic and copies ran while one was open for 2% -> 0% of each run, Pallas kernels for 0% -> 0%
where the time goes in v1:
time: 39 us; the launch traced here: 38.6 us
  Pallas kernels  36 us (92%)
  local copies, waits for them, and re-layouts  1.78 us (5%)
  between operations  0.88 us (2%)
    pallas_call x1, Pallas kernels, solve_direct(): pl.pallas_call(functools.partial(solve_kernel, n_py, n_pz), out_shape=jax...  19.8 us
    pallas_call x1, Pallas kernels, spread(): pl.pallas_call(spread_kernel, out_shape=jax.ShapeDtypeStruct((node_blocks...  8.34 us
    pallas_call x1, Pallas kernels, collect(): pl.pallas_call(collect_kernel, out_shape=jax.ShapeDtypeStruct((3, PB_DEV...  7.85 us
    unnamed x22, local copies, waits for them, and re-layouts  1.78 us

profile of v1, /device:TPU:0, one launch (start us, length us, event | category | flops | bytes accessed | tf_op | source)
XLA Modules:
  0.0 38.6 jit_solution(12638008036553341398)
XLA Ops:
  0.0 0.0 copy-start.6
  0.0 0.0 copy-start.9
  0.0 0.0 copy-start.10
  0.0 0.0 copy-start.7
  0.0 0.0 copy-start.8
  0.0 0.0 copy-start.4
  0.0 0.0 copy-start.5
  0.0 0.0 copy-start.2
  0.1 0.0 copy-start.3
  0.8 8.3 %spread.1 = f32[96,8,64]{2,1,0:T(8,128)} custom-call(s32[256]{0:T(256)} %part.3, s32[256]{0:T(256)} %node.3, s32[1]{0:T(128)S(6)} %copy.15.count, bf16[3,4096]{1,0:T(4,128)(2,1)} %parts_ref.1, bf16[256,64,128]{2,1,0:T(8,128)(2,1)} %w_ref.3), custom_call_target="tpu_custom_call" | custom-call | tf_op jit(solution)/shard_map/spread/pallas_call | solution.py:122
  9.2 0.0 copy-done.6
  9.2 0.0 copy-done.9
  9.2 0.0 copy-done.10
  9.2 0.0 copy-done.7
  9.2 0.0 copy-done.8
  9.2 0.0 copy-done.4
  9.2 0.0 copy-done.5
  9.2 0.0 copy-done.2
  9.2 0.0 copy-done.3
  9.2 0.0 copy-start.1
  9.2 1.0 %copy-done.1 = f32[96,8,64]{2,1,0:T(8,128)S(1)} copy-done((f32[96,8,64]{2,1,0:T(8,128)S(1)}, f32[96,8,64]{2,1,0:T(8,128)}, u32[]{:S(2)}) %copy-start.1) | copy-done | bytes 196632
  10.2 19.8 %solve.1 = f32[768,64]{1,0:T(8,128)S(1)} custom-call(f32[768,64]{1,0:T(8,128)S(1)} %bitcast.3, bf16[2,256,384]{2,1,0:T(8,128)(2,1)S(1)} %copy-done.3, bf16[2,256,384]{2,1,0:T(8,128)(2,1)S(1)} %copy-done.2, bf16[512,256]{1,0:T(8,128)(2,1)S(1)} %copy-done.5, bf16[512,256]{1,0:T(8,128)(2,1)S(1)} %copy-done.4, bf16[128,256]{1,0:T(8,128)(2,1)S(1)} %copy-done.8, ...), custom_call_target="tpu_custom_call" | custom-call | tf_op jit(solution)/shard_map/solve/pallas_call | solution.py:387
  30.0 0.0 copy-start
  30.0 0.7 %copy-done = f32[768,64]{1,0:T(8,128)} copy-done((f32[768,64]{1,0:T(8,128)}, f32[768,64]{1,0:T(8,128)S(1)}, u32[]{:S(2)}) %copy-start) | copy-done | bytes 196632
  30.8 7.9 %collect.1 = f32[3,4096]{1,0:T(4,128)} custom-call(s32[256]{0:T(256)} %part.3, s32[256]{0:T(256)} %node.3, s32[1]{0:T(128)S(6)} %copy.15.count, f32[96,8,64]{2,1,0:T(8,128)} %bitcast.2, bf16[256,64,128]{2,1,0:T(8,128)(2,1)} %w_ref.3), custom_call_target="tpu_custom_call" | custom-call | tf_op jit(solution)/shard_map/collect/pallas_call | solution.py:168
Async XLA Ops:
  0.0 9.2 %copy-start.6 = (f32[8,32,128]{2,1,0:T(8,128)S(1)}, f32[8,32,128]{2,1,0:T(8,128)}, u32[]{:S(2)}) copy-start(f32[8,32,128]{2,1,0:T(8,128)} %constant.26.clone.small) | copy-start | bytes 393220
  0.0 9.2 %copy-start.9 = (bf16[128,128]{1,0:T(8,128)(2,1)S(1)}, bf16[128,128]{1,0:T(8,128)(2,1)}, u32[]{:S(2)}) copy-start(bf16[128,128]{1,0:T(8,128)(2,1)} %constant.25.clone.back_l) | copy-start | bytes 98308
  0.0 9.2 %copy-start.10 = (bf16[128,128]{1,0:T(8,128)(2,1)S(1)}, bf16[128,128]{1,0:T(8,128)(2,1)}, u32[]{:S(2)}) copy-start(bf16[128,128]{1,0:T(8,128)(2,1)} %constant.24.clone.back_h) | copy-start | bytes 98308
  0.0 9.2 %copy-start.7 = (bf16[128,256]{1,0:T(8,128)(2,1)S(1)}, bf16[128,256]{1,0:T(8,128)(2,1)}, u32[]{:S(2)}) copy-start(bf16[128,256]{1,0:T(8,128)(2,1)} %constant.23.clone.fwd_l) | copy-start | bytes 196612
  0.0 9.2 %copy-start.8 = (bf16[128,256]{1,0:T(8,128)(2,1)S(1)}, bf16[128,256]{1,0:T(8,128)(2,1)}, u32[]{:S(2)}) copy-start(bf16[128,256]{1,0:T(8,128)(2,1)} %constant.22.clone.fwd_h) | copy-start | bytes 196612
  0.0 9.2 %copy-start.4 = (bf16[512,256]{1,0:T(8,128)(2,1)S(1)}, bf16[512,256]{1,0:T(8,128)(2,1)}, u32[]{:S(2)}) copy-start(bf16[512,256]{1,0:T(8,128)(2,1)} %constant.21.clone.far_l) | copy-start | bytes 786436
  0.0 9.2 %copy-start.5 = (bf16[512,256]{1,0:T(8,128)(2,1)S(1)}, bf16[512,256]{1,0:T(8,128)(2,1)}, u32[]{:S(2)}) copy-start(bf16[512,256]{1,0:T(8,128)(2,1)} %constant.20.clone.far_h) | copy-start | bytes 786436
  0.0 9.2 %copy-start.2 = (bf16[2,256,384]{2,1,0:T(8,128)(2,1)S(1)}, bf16[2,256,384]{2,1,0:T(8,128)(2,1)}, u32[]{:S(2)}) copy-start(bf16[2,256,384]{2,1,0:T(8,128)(2,1)} %constant.19.clone.xl_ref) | copy-start | bytes 1179652
  0.1 9.2 %copy-start.3 = (bf16[2,256,384]{2,1,0:T(8,128)(2,1)S(1)}, bf16[2,256,384]{2,1,0:T(8,128)(2,1)}, u32[]{:S(2)}) copy-start(bf16[2,256,384]{2,1,0:T(8,128)(2,1)} %constant.18.clone.xh_ref) | copy-start | bytes 1179652
  9.2 1.0 %copy-start.1 = (f32[96,8,64]{2,1,0:T(8,128)S(1)}, f32[96,8,64]{2,1,0:T(8,128)}, u32[]{:S(2)}) copy-start(f32[96,8,64]{2,1,0:T(8,128)} %spread.1) | copy-start | bytes 589828
  30.0 0.7 %copy-start = (f32[768,64]{1,0:T(8,128)}, f32[768,64]{1,0:T(8,128)S(1)}, u32[]{:S(2)}) copy-start(f32[768,64]{1,0:T(8,128)S(1)} %solve.1) | copy-start | bytes 589828

commit v2 on v1

--- a/solution.py
+++ b/solution.py
@@ -17,7 +17,7 @@
 PB_DEV = 32
 ROWS = 8
 CHUNK = 32
-GROUP = 16
+GROUP = 4
 MESH = pl.DeviceIdType.MESH
 f32 = jnp.float32
 bf16 = jnp.bfloat16
@@ -93,91 +93,102 @@
     return lax.dot_general(a, b, (dims, ((), ())), preferred_element_type=f32)
 
 
-def spread_kernel(part, node, count, parts_ref, w_ref, out_ref):
-    step = pl.program_id(0)
-
-    @pl.when(step == 0)
-    def _():
-        out_ref[...] = jnp.zeros_like(out_ref)
-
-    def group(g, carry):
-        sums = []
-        for i in range(GROUP):
-            p = g * GROUP + i
-            slot = step * CHUNK + p
-            start = pl.multiple_of(part[slot] * BP, BP)
-            picked = parts_ref[:, pl.ds(start, BP)]
-            got = dot(picked, w_ref[p], ((1,), (1,)))
-            sums.append(jnp.where(slot < count[0], got, 0.0))
-        for i in range(GROUP):
-            j = node[step * CHUNK + g * GROUP + i]
-            out_ref[j, 0:3, :] += sums[i]
+def left_half(shape):
+    return lax.broadcasted_iota(jnp.int32, shape, 1) < BN
+
+
+def spread_kernel(part, node, count, parts_ref, w_ref, out_ref, near_ref, parts, sems):
+    chunks = w_ref.shape[0] // CHUNK
+
+    def fetch(k):
+        here = pl.ds(k * CHUNK, CHUNK)
+        return pltpu.make_async_copy(w_ref.at[here], near_ref.at[here], sems.at[k])
+
+    for k in range(chunks):
+        fetch(k).start()
+    out_ref[...] = jnp.zeros_like(out_ref)
+    parts[...] = jnp.zeros_like(parts)
+    for b in range(PB_DEV):
+        parts[b, 0:3, :] = parts_ref[:, b * BP : (b + 1) * BP].astype(f32)
+    left = left_half((ROWS, 128))
+
+    def chunk(k, carry):
+        fetch(k).wait()
+        base = k * CHUNK
+        for g in range(CHUNK // GROUP):
+            first = base + g * GROUP
+            picked = jnp.concatenate([parts[part[first + i]] for i in range(GROUP)], axis=0)
+            tiles = near_ref[pl.ds(first, GROUP)].reshape(GROUP * BN, BP)
+            got = dot(picked.astype(bf16), tiles, ((1,), (1,)))
+            for i in range(GROUP):
+                keep = jnp.logical_and(left if i % 2 == 0 else ~left, first + i < count[0])
+                lanes = i // 2 * 128
+                own = got[i * ROWS : (i + 1) * ROWS, lanes : lanes + 128]
+                out_ref[node[first + i]] += jnp.where(keep, own, 0.0)
         return carry
 
-    lax.fori_loop(0, CHUNK // GROUP, group, 0)
+    lax.fori_loop(0, chunks, chunk, 0)
 
 
 def spread(vort_p, weights, part, node, counts, node_blocks):
-    slots = weights.shape[0]
+    smem = pl.BlockSpec(memory_space=pltpu.SMEM)
+    vmem = pl.BlockSpec(memory_space=pltpu.VMEM)
     return pl.pallas_call(
         spread_kernel,
-        out_shape=jax.ShapeDtypeStruct((node_blocks, ROWS, BN), f32),
-        grid_spec=pltpu.PrefetchScalarGridSpec(
-            num_scalar_prefetch=3,
-            grid=(slots // CHUNK,),
-            in_specs=[
-                pl.BlockSpec(vort_p.shape, lambda i, *_: (0, 0)),
-                pl.BlockSpec((CHUNK, BN, BP), lambda i, *_: (i, 0, 0)),
-            ],
-            out_specs=pl.BlockSpec((node_blocks, ROWS, BN), lambda i, *_: (0, 0, 0)),
+        out_shape=(
+            jax.ShapeDtypeStruct((node_blocks, ROWS, 2 * BN), f32),
+            jax.ShapeDtypeStruct(weights.shape, weights.dtype),
         ),
+        in_specs=[smem, smem, smem, vmem, pl.BlockSpec(memory_space=pltpu.HBM)],
+        out_specs=(vmem, vmem),
+        scratch_shapes=[
+            pltpu.VMEM((PB_DEV, ROWS, BP), f32),
+            pltpu.SemaphoreType.DMA((weights.shape[0] // CHUNK,)),
+        ],
+        compiler_params=pltpu.CompilerParams(vmem_limit_bytes=48 * 2**20),
         name="spread",
     )(part, node, counts, vort_p, weights)
 
 
-def collect_kernel(part, node, count, vel_ref, w_ref, out_ref, sums_ref):
-    step = pl.program_id(0)
-
-    @pl.when(step == 0)
-    def _():
-        sums_ref[...] = jnp.zeros_like(sums_ref)
-
-    def group(g, carry):
-        sums = []
-        for i in range(GROUP):
-            p = g * GROUP + i
-            slot = step * CHUNK + p
-            chosen = vel_ref[node[slot]].astype(bf16)
-            got = dot(chosen, w_ref[p])
-            sums.append(jnp.where(slot < count[0], got, 0.0))
-        for i in range(GROUP):
-            b = part[step * CHUNK + g * GROUP + i]
-            sums_ref[b] += sums[i]
+def collect_kernel(part, node, count, vel_ref, w_ref, out_ref, sums):
+    sums[...] = jnp.zeros_like(sums)
+    left = left_half((ROWS, 128))
+    zero = jnp.zeros((ROWS, 128), f32)
+
+    def chunk(k, carry):
+        for g in range(CHUNK // GROUP):
+            first = k * CHUNK + g * GROUP
+            rows = []
+            for i in range(GROUP):
+                slot = first + i
+                keep = jnp.logical_and(left if i % 2 == 0 else ~left, slot < count[0])
+                own = jnp.where(keep, vel_ref[node[slot]], 0.0)
+                rows.append(
+                    jnp.concatenate(
+                        [own if h == i // 2 else zero for h in range(GROUP // 2)], axis=1
+                    )
+                )
+            chosen = jnp.concatenate(rows, axis=0).astype(bf16)
+            got = dot(chosen, w_ref[pl.ds(first, GROUP)].reshape(GROUP * BN, BP))
+            for i in range(GROUP):
+                sums[part[first + i]] += got[i * ROWS : (i + 1) * ROWS]
         return carry
 
-    lax.fori_loop(0, CHUNK // GROUP, group, 0)
-
-    @pl.when(step == pl.num_programs(0) - 1)
-    def _():
-        for b in range(PB_DEV):
-            out_ref[:, b * BP : (b + 1) * BP] = sums_ref[b, 0:3, :]
+    lax.fori_loop(0, w_ref.shape[0] // CHUNK, chunk, 0)
+    for b in range(PB_DEV):
+        out_ref[:, b * BP : (b + 1) * BP] = sums[b, 0:3, :]
 
 
 def collect(vel, weights, part, node, counts):
-    slots = weights.shape[0]
+    smem = pl.BlockSpec(memory_space=pltpu.SMEM)
+    vmem = pl.BlockSpec(memory_space=pltpu.VMEM)
     return pl.pallas_call(
         collect_kernel,
         out_shape=jax.ShapeDtypeStruct((3, PB_DEV * BP), f32),
-        grid_spec=pltpu.PrefetchScalarGridSpec(
-            num_scalar_prefetch=3,
-            grid=(slots // CHUNK,),
-            in_specs=[
-                pl.BlockSpec(vel.shape, lambda i, *_: (0, 0, 0)),
-                pl.BlockSpec((CHUNK, BN, BP), lambda i, *_: (i, 0, 0)),
-            ],
-            out_specs=pl.BlockSpec((3, PB_DEV * BP), lambda i, *_: (0, 0)),
-            scratch_shapes=[pltpu.VMEM((PB_DEV, ROWS, BP), f32)],
-        ),
+        in_specs=[smem, smem, smem, vmem, vmem],
+        out_specs=vmem,
+        scratch_shapes=[pltpu.VMEM((PB_DEV, ROWS, BP), f32)],
+        compiler_params=pltpu.CompilerParams(vmem_limit_bytes=24 * 2**20),
         name="collect",
     )(part, node, counts, vel, weights)
 
@@ -266,8 +277,11 @@
     rows = devices * ROWS
     per_row = NX // BN
     cells = CY * CZ
-    me = lax.axis_index("py") * n_pz + lax.axis_index("pz")
+    my_y, my_z = lax.axis_index("py"), lax.axis_index("pz")
+    me = my_y * n_pz + my_z
     barrier = pltpu.get_barrier_semaphore()
+    recv_a[...] = jnp.zeros_like(recv_a)
+    recv_b[...] = jnp.zeros_like(recv_b)
 
     def greet(k, carry):
         other = lax.rem(me + k, devices)
@@ -278,35 +292,41 @@
 
     lax.fori_loop(1, devices, greet, 0)
 
+    sent = pl.ds(0, local)
+
     def exchange(send, recv, phase):
-        def copy(k, carry):
-            other = lax.rem(me + k, devices)
+        for k in range(1, devices):
+            to_y = lax.rem(my_y + k // n_pz, n_py)
+            to_z = lax.rem(my_z + k % n_pz, n_pz)
             pltpu.make_async_remote_copy(
-                src_ref=send.at[other],
-                dst_ref=recv.at[me],
+                src_ref=send.at[to_y * n_pz + to_z, sent],
+                dst_ref=recv.at[me, sent],
                 send_sem=send_sem.at[phase],
                 recv_sem=recv_sem.at[phase],
-                device_id=(other // n_pz, lax.rem(other, n_pz)),
+                device_id=(to_y, to_z),
                 device_id_type=MESH,
             ).start()
-            return carry
-
-        lax.fori_loop(1, devices, copy, 0)
 
     def finish(send, recv, phase):
         many = pl.ds(0, devices - 1)
-        pltpu.make_async_copy(recv.at[many], recv.at[many], recv_sem.at[phase]).wait()
+        pltpu.make_async_copy(recv.at[many, sent], recv.at[many, sent], recv_sem.at[phase]).wait()
 
     def drain(send, phase):
         many = pl.ds(0, devices - 1)
-        pltpu.make_async_copy(send.at[many], send.at[many], send_sem.at[phase]).wait()
-
+        pltpu.make_async_copy(send.at[many, sent], send.at[many, sent], send_sem.at[phase]).wait()
+
+    left = left_half((cells, 128))
     lines = []
     for c in range(3):
-        pieces = [
-            grid_ref[pl.ds(xb * ROWS + c, cells, stride=per_row * ROWS), :]
-            for xb in range(per_row)
-        ]
+        pieces = []
+        for xb in range(0, per_row, 2):
+            first, second = (
+                grid_ref[pl.ds((xb + h) * ROWS + c, cells, stride=per_row * ROWS), :]
+                for h in (0, 1)
+            )
+            first += pltpu.roll(first, BN, 1)
+            second += pltpu.roll(second, BN, 1)
+            pieces.append(jnp.where(left, first, second))
         lines.append(jnp.concatenate(pieces, axis=1))
     vort = jnp.concatenate(lines, axis=0)
     low = jnp.concatenate([vort, jnp.zeros((80, NX), f32)], axis=0)
@@ -371,10 +391,12 @@
         grid += dot(high, xh_ref[k]) + (dot(rest, xh_ref[k]) + dot(high, xl_ref[k]))
     grid = grid.astype(bf16).astype(f32)
     for c in range(3):
-        for xb in range(per_row):
-            out_ref[pl.ds(xb * ROWS + c, cells, stride=per_row * ROWS), :] = grid[
-                c * cells : (c + 1) * cells, xb * BN : (xb + 1) * BN
-            ]
+        for xb in range(0, per_row, 2):
+            piece = grid[c * cells : (c + 1) * cells, xb * BN : (xb + 2) * BN]
+            other = pltpu.roll(piece, BN, 1)
+            for h, both in ((0, jnp.where(left, piece, other)), (1, jnp.where(left, other, piece))):
+                where = pl.ds((xb + h) * ROWS + c, cells, stride=per_row * ROWS)
+                out_ref[where, :] = both
     drain(send_b, 1)
 
 
@@ -383,7 +405,7 @@
     vmem = pl.BlockSpec(memory_space=pltpu.VMEM)
     block = pltpu.VMEM((devices, ROWS, 128), f32)
     consts = tables(n_py, n_pz)
-    flat = sums.reshape(-1, BN)
+    flat = sums.reshape(-1, 2 * BN)
     out = pl.pallas_call(
         functools.partial(solve_kernel, n_py, n_pz),
         out_shape=jax.ShapeDtypeStruct(flat.shape, f32),
@@ -410,7 +432,8 @@
     node_blocks = sums.shape[0]
     y_cells, z_cells = CY * n_py, CZ * n_pz
     x_modes = NX // 2
-    vort_grid = sums[:, :3].transpose(1, 0, 2).reshape(3, CZ, CY, NX)
+    sums = sums[:, :3, :BN] + sums[:, :3, BN:]
+    vort_grid = sums.transpose(1, 0, 2).reshape(3, CZ, CY, NX)
     angle_fwd = twiddle(jnp.arange(NX), jnp.arange(x_modes), NX)
     x_forward = jnp.stack([jnp.cos(angle_fwd), -jnp.sin(angle_fwd)], 1)
     angle_inv = twiddle(jnp.arange(x_modes), jnp.arange(NX), NX)
@@ -448,18 +471,19 @@
         precision=highest,
     )
     vel_nodes = vel_grid.astype(bf16).astype(f32).reshape(3, node_blocks, BN).transpose(1, 0, 2)
+    vel_nodes = jnp.concatenate([vel_nodes, vel_nodes], axis=2)
     return jnp.pad(vel_nodes, ((0, 0), (0, ROWS - 3), (0, 0)))
 
 
 def per_device(vort_p, pair_weights, pair_part, pair_node, counts):
     n_py, n_pz = lax.axis_size("py"), lax.axis_size("pz")
     node_blocks = NX * CY * CZ // BN
-    sums = spread(vort_p, pair_weights, pair_part, pair_node, counts, node_blocks)
+    sums, near = spread(vort_p, pair_weights, pair_part, pair_node, counts, node_blocks)
     x_modes = NX // 2
     devices = n_py * n_pz
     direct = devices <= 32 and x_modes % devices == 0 and x_modes // devices <= ROWS
     vel = (solve_direct if direct else solve_staged)(sums, n_py, n_pz)
-    return collect(vel, pair_weights, pair_part, pair_node, counts)
+    return collect(vel, near, pair_part, pair_node, counts)
 
 
 def solution(mesh):

time: 39 us -> 29.9 us (0.77)
  Pallas kernels: 36 us -> 26.7 us
    pallas_call x1, Pallas kernels: 7.85 us -> 3.24 us  [collect(): pl.pallas_call(collect_kernel, out_shape=jax.ShapeDtypeStruct((3, PB_DEV...]
    pallas_call x1, Pallas kernels: 8.34 us -> 4.17 us  [spread(): pl.pallas_call(spread_kernel, out_shape=(jax.ShapeDtypeStruct((node_block...]
    pallas_call x1, Pallas kernels: 19.8 us -> 19.3 us  [solve_direct(): pl.pallas_call(functools.partial(solve_kernel, n_py, n_pz), out_shape=jax...]
    unnamed x22 -> x24, local copies, waits for them, and re-layouts: 1.78 us -> 2.15 us
where the time goes in v2:
time: 29.9 us; the launch traced here: 29.8 us
  Pallas kernels  26.7 us (89%)
  local copies, waits for them, and re-layouts  2.15 us (7%)
  between operations  0.88 us (3%)
    pallas_call x1, Pallas kernels, solve_direct(): pl.pallas_call(functools.partial(solve_kernel, n_py, n_pz), out_shape=jax...  19.3 us
    pallas_call x1, Pallas kernels, spread(): pl.pallas_call(spread_kernel, out_shape=(jax.ShapeDtypeStruct((node_block...  4.17 us
    pallas_call x1, Pallas kernels, collect(): pl.pallas_call(collect_kernel, out_shape=jax.ShapeDtypeStruct((3, PB_DEV...  3.24 us
    unnamed x24, local copies, waits for them, and re-layouts  2.15 us

profile of v2, /device:TPU:0, one launch (start us, length us, event | category | flops | bytes accessed | tf_op | source)
XLA Modules:
  0.0 29.8 jit_solution(1017297414894646104)
XLA Ops:
  0.0 0.0 copy-start.4
  0.0 0.0 copy-start.5
  0.0 0.0 copy-start.6
  0.0 0.0 copy-start.2
  0.0 0.0 copy-start.3
  0.0 0.0 copy-start
  0.0 0.0 copy-start.1
  0.8 0.0 copy-start.7
  0.8 0.7 %copy-done.7 = bf16[3,4096]{1,0:T(4,128)(2,1)S(1)} copy-done((bf16[3,4096]{1,0:T(4,128)(2,1)S(1)}, bf16[3,4096]{1,0:T(4,128)(2,1)}, u32[]{:S(2)}) %copy-start.7) | copy-done | bytes 24600
  1.6 0.0 copy-start.10
  1.6 0.7 %copy-done.10 = s32[256]{0:T(256)S(1)} copy-done((s32[256]{0:T(256)S(1)}, s32[256]{0:T(256)}, u32[]{:S(2)}) %copy-start.10) | copy-done | bytes 1048
  2.2 0.0 copy-start.11
  2.2 0.7 %copy-done.11 = s32[256]{0:T(256)S(1)} copy-done((s32[256]{0:T(256)S(1)}, s32[256]{0:T(256)}, u32[]{:S(2)}) %copy-start.11) | copy-done | bytes 1048
  2.9 0.0 copy-start.8
  2.9 0.0 copy-start.9
  2.9 4.2 %spread.1 = (f32[96,8,128]{2,1,0:T(8,128)S(1)}, bf16[256,64,128]{2,1,0:T(8,128)(2,1)S(1)}) custom-call(s32[256]{0:T(256)S(1)} %copy-done.10, s32[256]{0:T(256)S(1)} %copy-done.11, s32[1]{0:T(128)S(6)} %copy.15.count, bf16[3,4096]{1,0:T(4,128)(2,1)S(1)} %copy-done.7, bf16[256,64,128]{2,1,0:T(8,128)(2,1)} %w_ref.1), custom_call_target="tpu_custom_call" | custom-call | tf_op jit(solution)/shard_map/spread/pallas_call | solution.py:136
  7.1 0.0 copy-done.4
  7.1 0.0 copy-done.5
  7.1 0.0 copy-done.6
  7.1 0.0 copy-done.2
  7.1 0.0 copy-done.3
  7.2 0.0 copy-done
  7.2 0.0 copy-done.1
  7.2 0.0 copy-done.8
  7.2 0.0 copy-done.9
  7.2 19.3 %solve.1 = f32[768,128]{1,0:T(8,128)S(1)} custom-call(f32[768,128]{1,0:T(8,128)S(1)} %bitcast.3, bf16[2,256,384]{2,1,0:T(8,128)(2,1)S(1)} %copy-done.1, bf16[2,256,384]{2,1,0:T(8,128)(2,1)S(1)} %copy-done, bf16[512,256]{1,0:T(8,128)(2,1)S(1)} %copy-done.3, bf16[512,256]{1,0:T(8,128)(2,1)S(1)} %copy-done.2, bf16[128,256]{1,0:T(8,128)(2,1)S(1)} %copy-done.6, ...), custom_call_target="tpu_custom_call" | custom-call | tf_op jit(solution)/shard_map/solve/pallas_call | solution.py:409
  26.5 3.2 %collect.1 = f32[3,4096]{1,0:T(4,128)} custom-call(s32[256]{0:T(256)S(1)} %copy-done.10, s32[256]{0:T(256)S(1)} %copy-done.11, s32[1]{0:T(128)S(6)} %copy.15.count, f32[96,8,128]{2,1,0:T(8,128)S(1)} %bitcast.2, bf16[256,64,128]{2,1,0:T(8,128)(2,1)S(1)} %get-tuple-element.8.w_ref), custom_call_target="tpu_custom_call" | custom-call | tf_op jit(solution)/shard_map/collect/pallas_call | solution.py:185
Async XLA Ops:
  0.0 7.1 %copy-start.4 = (f32[8,32,128]{2,1,0:T(8,128)S(1)}, f32[8,32,128]{2,1,0:T(8,128)}, u32[]{:S(2)}) copy-start(f32[8,32,128]{2,1,0:T(8,128)} %constant.26.clone.small) | copy-start | bytes 393220
  0.0 7.1 %copy-start.5 = (bf16[128,256]{1,0:T(8,128)(2,1)S(1)}, bf16[128,256]{1,0:T(8,128)(2,1)}, u32[]{:S(2)}) copy-start(bf16[128,256]{1,0:T(8,128)(2,1)} %constant.23.clone.fwd_l) | copy-start | bytes 196612
  0.0 7.1 %copy-start.6 = (bf16[128,256]{1,0:T(8,128)(2,1)S(1)}, bf16[128,256]{1,0:T(8,128)(2,1)}, u32[]{:S(2)}) copy-start(bf16[128,256]{1,0:T(8,128)(2,1)} %constant.22.clone.fwd_h) | copy-start | bytes 196612
  0.0 7.1 %copy-start.2 = (bf16[512,256]{1,0:T(8,128)(2,1)S(1)}, bf16[512,256]{1,0:T(8,128)(2,1)}, u32[]{:S(2)}) copy-start(bf16[512,256]{1,0:T(8,128)(2,1)} %constant.21.clone.far_l) | copy-start | bytes 786436
  0.0 7.1 %copy-start.3 = (bf16[512,256]{1,0:T(8,128)(2,1)S(1)}, bf16[512,256]{1,0:T(8,128)(2,1)}, u32[]{:S(2)}) copy-start(bf16[512,256]{1,0:T(8,128)(2,1)} %constant.20.clone.far_h) | copy-start | bytes 786436
  0.0 7.1 %copy-start = (bf16[2,256,384]{2,1,0:T(8,128)(2,1)S(1)}, bf16[2,256,384]{2,1,0:T(8,128)(2,1)}, u32[]{:S(2)}) copy-start(bf16[2,256,384]{2,1,0:T(8,128)(2,1)} %constant.19.clone.xl_ref) | copy-start | bytes 1179652
  0.0 7.1 %copy-start.1 = (bf16[2,256,384]{2,1,0:T(8,128)(2,1)S(1)}, bf16[2,256,384]{2,1,0:T(8,128)(2,1)}, u32[]{:S(2)}) copy-start(bf16[2,256,384]{2,1,0:T(8,128)(2,1)} %constant.18.clone.xh_ref) | copy-start | bytes 1179652
  0.8 0.8 %copy-start.7 = (bf16[3,4096]{1,0:T(4,128)(2,1)S(1)}, bf16[3,4096]{1,0:T(4,128)(2,1)}, u32[]{:S(2)}) copy-start(bf16[3,4096]{1,0:T(4,128)(2,1)} %parts_ref.1) | copy-start | bytes 73732
  1.6 0.7 %copy-start.10 = (s32[256]{0:T(256)S(1)}, s32[256]{0:T(256)}, u32[]{:S(2)}) copy-start(s32[256]{0:T(256)} %part.3) | copy-start | bytes 3076
  2.2 0.7 %copy-start.11 = (s32[256]{0:T(256)S(1)}, s32[256]{0:T(256)}, u32[]{:S(2)}) copy-start(s32[256]{0:T(256)} %node.3) | copy-start | bytes 3076
  2.9 4.3 %copy-start.8 = (bf16[128,128]{1,0:T(8,128)(2,1)S(1)}, bf16[128,128]{1,0:T(8,128)(2,1)}, u32[]{:S(2)}) copy-start(bf16[128,128]{1,0:T(8,128)(2,1)} %constant.25.clone.back_l) | copy-start | bytes 98308
  2.9 4.3 %copy-start.9 = (bf16[128,128]{1,0:T(8,128)(2,1)S(1)}, bf16[128,128]{1,0:T(8,128)(2,1)}, u32[]{:S(2)}) copy-start(bf16[128,128]{1,0:T(8,128)(2,1)} %constant.24.clone.back_h) | copy-start | bytes 98308

commit v3 on v2

--- a/solution.py
+++ b/solution.py
@@ -254,24 +254,32 @@
 def solve_kernel(
     n_py,
     n_pz,
-    grid_ref,
-    xh_ref,
-    xl_ref,
-    far_h,
-    far_l,
-    fwd_h,
-    fwd_l,
-    back_h,
-    back_l,
-    small,
-    out_ref,
-    send_a,
-    recv_a,
-    send_b,
-    recv_b,
-    send_sem,
-    recv_sem,
+    count,
+    part_ref,
+    node_ref,
+    parts_ref,
+    w_ref,
+    *rest_refs,
 ):
+    n_consts = 9
+    consts, out_ref = rest_refs[:n_consts], rest_refs[n_consts]
+    held = rest_refs[n_consts + 1 : 2 * n_consts + 1]
+    (
+        near_ref,
+        vel_ref,
+        send_a,
+        recv_a,
+        send_b,
+        recv_b,
+        send_sem,
+        recv_sem,
+        parts,
+        picks,
+        pairs,
+        sems,
+        const_sems,
+    ) = rest_refs[2 * n_consts + 1 :]
+    xh_ref, xl_ref, far_h, far_l, fwd_h, fwd_l, back_h, back_l, small = held
     devices = n_py * n_pz
     local = NX // 2 // devices
     rows = devices * ROWS
@@ -279,7 +287,22 @@
     cells = CY * CZ
     my_y, my_z = lax.axis_index("py"), lax.axis_index("pz")
     me = my_y * n_pz + my_z
+    slots = w_ref.shape[0]
+    chunks = slots // CHUNK
     barrier = pltpu.get_barrier_semaphore()
+
+    def fetch(k):
+        here = pl.ds(k * CHUNK, CHUNK)
+        return pltpu.make_async_copy(w_ref.at[here], near_ref.at[here], sems.at[k])
+
+    for k in range(chunks):
+        fetch(k).start()
+    loads = [
+        pltpu.make_async_copy(c, h, const_sems.at[i]) for i, (c, h) in enumerate(zip(consts, held))
+    ]
+    for load in loads:
+        load.start()
+    vel_ref[...] = jnp.zeros_like(vel_ref)
     recv_a[...] = jnp.zeros_like(recv_a)
     recv_b[...] = jnp.zeros_like(recv_b)
 
@@ -295,8 +318,13 @@
     sent = pl.ds(0, local)
 
     def exchange(send, recv, phase):
-        for k in range(1, devices):
-            to_y = lax.rem(my_y + k // n_pz, n_py)
+        order = list(range(1, devices))
+        turns = [lax.rem(my_y + k, n_py) for k in range(n_py)]
+        if n_py == 4:
+            order = list(range(devices - n_pz)) + list(range(devices - n_pz + 1, devices))
+            turns = [3 - my_y, turns[2], 3 - turns[2], my_y]
+        for k in order:
+            to_y = turns[k // n_pz]
             to_z = lax.rem(my_z + k % n_pz, n_pz)
             pltpu.make_async_remote_copy(
                 src_ref=send.at[to_y * n_pz + to_z, sent],
@@ -315,18 +343,52 @@
         many = pl.ds(0, devices - 1)
         pltpu.make_async_copy(send.at[many, sent], send.at[many, sent], send_sem.at[phase]).wait()
 
+    picks[...] = jnp.zeros_like(picks)
+    parts[...] = jnp.zeros_like(parts)
+    for b in range(PB_DEV):
+        parts[b * ROWS : b * ROWS + 3, :] = parts_ref[:, b * BP : (b + 1) * BP].astype(f32)
+    row = lax.broadcasted_iota(jnp.int32, (PB_DEV, slots), 0)
+    chooser = jnp.where(row == part_ref[...], 1.0, 0.0).T.astype(bf16)
+    for c in range(3):
+        block = parts[pl.ds(c, PB_DEV, stride=ROWS), :].astype(bf16)
+        picks[pl.ds(c, slots, stride=ROWS), :] = dot(chooser, block)
+    near_half = left_half((ROWS, 128))
+
+    def chunk(k, carry):
+        fetch(k).wait()
+        for g in range(CHUNK // GROUP):
+            first = k * CHUNK + g * GROUP
+            picked = picks[pl.ds(first * ROWS, GROUP * ROWS), :]
+            tiles = near_ref[pl.ds(first, GROUP)].reshape(GROUP * BN, BP)
+            got = dot(picked.astype(bf16), tiles, ((1,), (1,)))
+            own = []
+            for i in range(GROUP):
+                lanes = i // 2 * 128
+                keep = near_half if i % 2 == 0 else ~near_half
+                piece = got[i * ROWS : (i + 1) * ROWS, lanes : lanes + 128]
+                own.append(jnp.where(keep, piece, 0.0))
+            pairs[pl.ds(first * ROWS, GROUP * ROWS), :] = jnp.concatenate(own, axis=0)
+        return carry
+
+    lax.fori_loop(0, chunks, chunk, 0)
+    for load in loads:
+        load.wait()
+    row = lax.broadcasted_iota(jnp.int32, (cells * per_row, slots), 0)
+    block = row % cells * per_row + row // cells
+    live = lax.broadcasted_iota(jnp.int32, (cells * per_row, slots), 1) < count[0]
+    hits = jnp.where((block == node_ref[...]) & live, 1.0, 0.0).astype(bf16)
     left = left_half((cells, 128))
     lines = []
     for c in range(3):
-        pieces = []
-        for xb in range(0, per_row, 2):
-            first, second = (
-                grid_ref[pl.ds((xb + h) * ROWS + c, cells, stride=per_row * ROWS), :]
-                for h in (0, 1)
+        high, rest = split(pairs[pl.ds(c, slots, stride=ROWS), :])
+        total = dot(hits, high) + dot(hits, rest)
+        total += pltpu.roll(total, BN, 1)
+        pieces = [
+            jnp.where(
+                left, total[xb * cells : (xb + 1) * cells], total[(xb + 1) * cells : (xb + 2) * cells]
             )
-            first += pltpu.roll(first, BN, 1)
-            second += pltpu.roll(second, BN, 1)
-            pieces.append(jnp.where(left, first, second))
+            for xb in range(0, per_row, 2)
+        ]
         lines.append(jnp.concatenate(pieces, axis=1))
     vort = jnp.concatenate(lines, axis=0)
     low = jnp.concatenate([vort, jnp.zeros((80, NX), f32)], axis=0)
@@ -396,35 +458,79 @@
             other = pltpu.roll(piece, BN, 1)
             for h, both in ((0, jnp.where(left, piece, other)), (1, jnp.where(left, other, piece))):
                 where = pl.ds((xb + h) * ROWS + c, cells, stride=per_row * ROWS)
-                out_ref[where, :] = both
+                vel_ref[where, :] = both
+
+    row = lax.broadcasted_iota(jnp.int32, (cells * per_row, slots), 0)
+    chooser = jnp.where(row == node_ref[...], 1.0, 0.0).T.astype(bf16)
+    for c in range(3):
+        block = vel_ref[pl.ds(c, cells * per_row, stride=ROWS), :].astype(bf16)
+        picks[pl.ds(c, slots, stride=ROWS), :] = dot(chooser, block)
+
+    def gather(k, carry):
+        for g in range(CHUNK // GROUP):
+            first = k * CHUNK + g * GROUP
+            lines = []
+            for i in range(GROUP):
+                keep = near_half if i % 2 == 0 else ~near_half
+                own = jnp.where(keep, picks[pl.ds((first + i) * ROWS, ROWS), :], 0.0)
+                zero = jnp.zeros((ROWS, 128), f32)
+                lines.append(
+                    jnp.concatenate(
+                        [own if h == i // 2 else zero for h in range(GROUP // 2)], axis=1
+                    )
+                )
+            chosen = jnp.concatenate(lines, axis=0).astype(bf16)
+            tiles = near_ref[pl.ds(first, GROUP)].reshape(GROUP * BN, BP)
+            pairs[pl.ds(first * ROWS, GROUP * ROWS), :] = dot(chosen, tiles)
+        return carry
+
+    lax.fori_loop(0, chunks, gather, 0)
+    row = lax.broadcasted_iota(jnp.int32, (PB_DEV, slots), 0)
+    live = lax.broadcasted_iota(jnp.int32, (PB_DEV, slots), 1) < count[0]
+    hits = jnp.where((row == part_ref[...]) & live, 1.0, 0.0).astype(bf16)
+    for c in range(3):
+        high, rest = split(pairs[pl.ds(c, slots, stride=ROWS), :])
+        out_ref[c] = dot(hits, high) + dot(hits, rest)
     drain(send_b, 1)
 
 
-def solve_direct(sums, n_py, n_pz):
+def solve_direct(vort_p, weights, part, node, counts, n_py, n_pz):
     devices = n_py * n_pz
+    node_blocks = NX * CY * CZ // BN
+    slots = weights.shape[0]
+    smem = pl.BlockSpec(memory_space=pltpu.SMEM)
     vmem = pl.BlockSpec(memory_space=pltpu.VMEM)
+    hbm = pl.BlockSpec(memory_space=pltpu.HBM)
     block = pltpu.VMEM((devices, ROWS, 128), f32)
     consts = tables(n_py, n_pz)
-    flat = sums.reshape(-1, 2 * BN)
+    consts = [jnp.asarray(t) for t in consts]
     out = pl.pallas_call(
         functools.partial(solve_kernel, n_py, n_pz),
-        out_shape=jax.ShapeDtypeStruct(flat.shape, f32),
-        in_specs=[vmem] * (1 + len(consts)),
+        out_shape=jax.ShapeDtypeStruct((3, PB_DEV, BP), f32),
+        in_specs=[smem, vmem, vmem, vmem, hbm] + [hbm] * len(consts),
         out_specs=vmem,
         scratch_shapes=[
+            *[pltpu.VMEM(t.shape, t.dtype) for t in consts],
+            pltpu.VMEM(weights.shape, weights.dtype),
+            pltpu.VMEM((node_blocks * ROWS, 2 * BN), f32),
             block,
             block,
             block,
             block,
             pltpu.SemaphoreType.DMA((2,)),
             pltpu.SemaphoreType.DMA((2,)),
+            pltpu.VMEM((PB_DEV * ROWS, BP), f32),
+            pltpu.VMEM((slots * ROWS, 128), f32),
+            pltpu.VMEM((slots * ROWS, 128), f32),
+            pltpu.SemaphoreType.DMA((slots // CHUNK,)),
+            pltpu.SemaphoreType.DMA((len(consts),)),
         ],
         compiler_params=pltpu.CompilerParams(
-            collective_id=0, has_side_effects=True, vmem_limit_bytes=32 * 2**20
+            collective_id=0, has_side_effects=True, vmem_limit_bytes=60 * 2**20
         ),
         name="solve",
-    )(flat, *[jnp.asarray(t) for t in consts])
-    return out.reshape(sums.shape)
+    )(counts, part[None], node[None], vort_p, weights, *consts)
+    return out.reshape(3, PB_DEV * BP)
 
 
 def solve_staged(sums, n_py, n_pz):
@@ -478,11 +584,11 @@
 def per_device(vort_p, pair_weights, pair_part, pair_node, counts):
     n_py, n_pz = lax.axis_size("py"), lax.axis_size("pz")
     node_blocks = NX * CY * CZ // BN
+    devices, x_modes = n_py * n_pz, NX // 2
+    if devices <= 32 and x_modes % devices == 0 and x_modes // devices <= ROWS:
+        return solve_direct(vort_p, pair_weights, pair_part, pair_node, counts, n_py, n_pz)
     sums, near = spread(vort_p, pair_weights, pair_part, pair_node, counts, node_blocks)
-    x_modes = NX // 2
-    devices = n_py * n_pz
-    direct = devices <= 32 and x_modes % devices == 0 and x_modes // devices <= ROWS
-    vel = (solve_direct if direct else solve_staged)(sums, n_py, n_pz)
+    vel = solve_staged(sums, n_py, n_pz)
     return collect(vel, near, pair_part, pair_node, counts)
 
 

time: 29.9 us -> 25.5 us (0.85)
  Pallas kernels: 26.7 us -> 23.1 us
  local copies, waits for them, and re-layouts: 2.15 us -> 1.46 us
    pallas_call x2 -> x0, Pallas kernels: 7.4 us -> none  [the longest x1 4.17 us: spread(): pl.pallas_call(spread_kernel, out_shape=(jax.ShapeDtypeStruct((node_block...]
    pallas_call x1, Pallas kernels: 19.3 us -> 23.1 us  [solve_direct(): pl.pallas_call(functools.partial(solve_kernel, n_py, n_pz), out_shape=jax...]
    unnamed x24 -> x1, local copies, waits for them, and re-layouts: 2.15 us -> 1.46 us
where the time goes in v3:
time: 25.5 us; the launch traced here: 25.2 us
  Pallas kernels  23.1 us (91%)
  local copies, waits for them, and re-layouts  1.46 us (6%)
  between operations  0.66 us (3%)
    pallas_call x1, Pallas kernels, solve_direct(): pl.pallas_call(functools.partial(solve_kernel, n_py, n_pz), out_shape=jax...  23.1 us
    unnamed x1, local copies, waits for them, and re-layouts  1.46 us

profile of v3, /device:TPU:0, one launch (start us, length us, event | category | flops | bytes accessed | tf_op | source)
XLA Modules:
  0.0 25.2 jit_solution(16608775270704185995)
XLA Ops:
  0.7 23.1 %solve.1 = f32[3,32,128]{2,1,0:T(8,128)} custom-call(s32[1]{0:T(128)S(6)} %copy.18.count, s32[1,256]{1,0:T(1,128)} %bitcast.7, s32[1,256]{1,0:T(1,128)} %bitcast.8, bf16[3,4096]{1,0:T(4,128)(2,1)} %parts_ref.1, bf16[256,64,128]{2,1,0:T(8,128)(2,1)} %w_ref.1, bf16[2,256,384]{2,1,0:T(8,128)(2,1)} %constant.18.clone.rest_refs_0_, ...), custom_call_target="tpu_custom_call" | custom-call | tf_op jit(solution)/shard_map/solve/pallas_call | solution.py:507
  23.8 1.5 %copy.17 = f32[1,3,32,128]{3,1,2,0:T(4,128)} copy(f32[1,3,32,128]{3,2,1,0:T(8,128)} %bitcast.6) | data formatting | bytes 98304
